TPU v7x, 512 devices: a whole 4x4x16 slice. The times are simulated.
512 devices in a mesh: fsdp: 64 (over z, y), tensor: 8 (over x, core).
Axes of the slice: x: 4, y: 4, z: 16, core: 2. Of those that a mesh axis runs over, the one named last changes fastest.
Arguments:
- grads: float32 [64, 1024, 1024], P(None, 'fsdp', 'tensor'), may hold values from -20 to 20
- block_slot: int32 [64], replicated, may hold values from 0 to 127, as said below
- stat_left: bfloat16 [128, 1024, 1024], P('fsdp', 'tensor'), may hold values from -6 to 6
- stat_right: bfloat16 [128, 1024, 1024], P('fsdp', 'tensor'), may hold values from -6 to 6
- root_left: bfloat16 [128, 1024, 1024], P('fsdp', 'tensor'), may hold values from -1 to 2
- root_right: bfloat16 [128, 1024, 1024], P('fsdp', None, 'tensor'), may hold values from -1 to 2
Outputs:
- directions: bfloat16 [64, 1024, 1024], P(None, 'fsdp', 'tensor')
- new_left: bfloat16 [128, 1024, 1024], P('fsdp', 'tensor')
- new_right: bfloat16 [128, 1024, 1024], P('fsdp', 'tensor')
Inputs may be any that keep to these rules, and one draw needn't show every extreme that they name: `block_slot`: the slots are distinct; slot s belongs to owner s // 2 along fsdp; in every draw some owner has all its 2 slots taken.
All inputs are finite; a program needn't handle non-finite values.
Results may differ from a plain program's by a relative error of at most 0.0057.
Values may be sent and summed in bfloat16 or wider, within the bound.
A program may use at most 64 MiB of HBM per device.

v0:
```python
import jax
import jax.numpy as jnp
from jax import lax
from jax.sharding import PartitionSpec as P

stat_decay = 0.95
graft_eps = 1e-06


def on_device(grads, block_slot, stat_left, stat_right, root_left, root_right):
    fsdp_count = lax.axis_size("fsdp")
    owner_index = lax.axis_index("fsdp")
    tensor_index = lax.axis_index("tensor")
    block_count, row_share, col_share = grads.shape
    slot_count = stat_left.shape[0]
    left_rows = stat_left.shape[1]
    slot_total = fsdp_count * slot_count
    slot_ids = jnp.arange(slot_total, dtype=jnp.int32)
    block_ids = jnp.arange(block_count, dtype=jnp.int32)
    slot_match = block_slot[None, :] == slot_ids[:, None]
    block_of_slot = jnp.sum(jnp.where(slot_match, block_ids[None, :], 0), axis=1)
    slot_used = jnp.any(slot_match, axis=1)
    mine_used = lax.dynamic_index_in_dim(
        slot_used.reshape(fsdp_count, slot_count), owner_index, 0, keepdims=False
    )
    wide_rows = lax.all_gather(grads.astype(jnp.bfloat16), "tensor", axis=2, tiled=True).astype(
        grads.dtype
    )
    picked = wide_rows[block_of_slot] * slot_used[:, None, None].astype(wide_rows.dtype)
    arrived = lax.all_to_all(
        picked.reshape(fsdp_count, slot_count, row_share, wide_rows.shape[2]).astype(jnp.bfloat16),
        "fsdp",
        split_axis=0,
        concat_axis=2,
        tiled=True,
    ).astype(jnp.float32)
    full_block = arrived[0]
    col_slab = lax.dynamic_slice_in_dim(full_block, tensor_index * col_share, col_share, 2)
    row_block = lax.dynamic_slice_in_dim(full_block, tensor_index * left_rows, left_rows, 1)
    left_prod = jnp.einsum("srk,sck->src", row_block, full_block, precision=lax.Precision.HIGHEST)
    right_prod = jnp.einsum("skr,skc->src", col_slab, full_block, precision=lax.Precision.HIGHEST)
    keep_mask = mine_used[:, None, None]
    left_old = stat_left.astype(jnp.float32)
    right_old = stat_right.astype(jnp.float32)
    new_left = jnp.where(
        keep_mask, stat_decay * left_old + (1.0 - stat_decay) * left_prod, left_old
    ).astype(jnp.bfloat16)
    new_right = jnp.where(
        keep_mask, stat_decay * right_old + (1.0 - stat_decay) * right_prod, right_old
    ).astype(jnp.bfloat16)
    grad_half = full_block.astype(jnp.bfloat16)
    half_right = jnp.einsum(
        "sik,skj->sij", grad_half, root_right, preferred_element_type=jnp.float32
    ).astype(jnp.bfloat16)
    precond = jnp.einsum(
        "snk,skj->snj",
        lax.all_gather(root_left, "tensor", axis=1, tiled=True),
        half_right,
        preferred_element_type=jnp.float32,
    )
    dir_part = jnp.sum(precond * precond, axis=(1, 2))
    grad_part = jnp.sum(col_slab * col_slab, axis=(1, 2))
    grad_sq, dir_sq = lax.psum((grad_part, dir_part), "tensor")
    graft_scale = jnp.sqrt(grad_sq / (dir_sq + graft_eps))
    direction = (precond * graft_scale[:, None, None]).astype(jnp.bfloat16)
    send_back = direction.reshape(slot_count, fsdp_count, row_share, col_share)
    returned = lax.all_to_all(send_back, "fsdp", split_axis=1, concat_axis=0, tiled=True)
    by_slot = returned.reshape(slot_total, row_share, col_share)
    directions = by_slot[block_slot]
    return (directions, new_left, new_right)


def solution(mesh):
    placed = (
        P(None, "fsdp", "tensor"),
        P(),
        P("fsdp", "tensor", None),
        P("fsdp", "tensor", None),
        P("fsdp", "tensor", None),
        P("fsdp", None, "tensor"),
    )
    return jax.shard_map(
        on_device,
        mesh=mesh,
        in_specs=placed,
        out_specs=(P(None, "fsdp", "tensor"), P("fsdp", "tensor", None), P("fsdp", "tensor", None)),
        check_vma=False,
    )
```

profile of v0, /device:TPU:1, one launch (start us, length us, event | category | flops | bytes accessed | tf_op | source)
XLA Modules:
  0.0 341.3 jit_solution(14703830564393525873)
XLA Ops:
  7.2 1.8 convert_element_type.54
  9.1 0.7 fusion.11
  9.8 0.2 reduce_or.12
  10.0 0.7 select_reduce_fusion
  10.8 40.6 %all-gather.3.cloned.1.call-done = bf16[64,16,1024]{2,1,0:T(8,128)(2,1)} async-done(((bf16[64,16,128]{2,1,0:T(8,128)(2,1)}), bf16[64,16,1024]{2,1,0:T(8,128)(2,1)}) %all-gather.3.cloned.1.call-update) | async-done | bytes 2097168 | tf_op jit(solution)/shard_map/all_gather | solution.py:26
  51.4 4.0 %convert_element_type.55 = f32[64,16,1024]{2,1,0:T(8,128)} convert(bf16[64,16,1024]{2,1,0:T(8,128)(2,1)} %all-gather.3.cloned.1.call-done) | non-fusion elementwise | flops 1048576 | bytes 6291456 | tf_op jit(solution)/shard_map/convert_element_type | solution.py:26
  55.4 6.5 %gather_fusion = f32[128,16,1024]{2,1,0:T(8,128)} fusion(f32[64,16,1024]{2,1,0:T(8,128)} %convert_element_type.55, s32[1024]{0:T(1024)S(1)} %pad_clamp_fusion.1), kind=kCustom, calls=%fused_computation | custom fusion | bytes 16777728 | tf_op jit(solution)/shard_map/gather | solution.py:29
  61.9 5.8 %multiply_convert_fusion = bf16[64,2,16,1024]{3,2,1,0:T(8,128)(2,1)} fusion(f32[64,2,16,1024]{3,2,1,0:T(8,128)} %bitcast.28, f32[64,2]{1,0:T(8,128)S(1)} %convert_element_type.56), kind=kLoop, calls=%fused_computation.2 | loop fusion | flops 4194304 | bytes 12583424 | tf_op jit(solution)/shard_map/convert_element_type | solution.py:31
  67.7 15.6 %all-to-all-start = ((bf16[64,2,16,1024]{3,2,1,0:T(8,128)(2,1)}), bf16[64,2,16,1024]{3,2,1,0:T(8,128)(2,1)}, u32[]{:S(2)}, u32[]{:S(2)}) async-start(bf16[64,2,16,1024]{3,2,1,0:T(8,128)(2,1)} %multiply_convert_fusion), calls=%async_computation | async-start | bytes 8388608 | tf_op jit(solution)/shard_map/all_to_all | solution.py:30
  83.4 0.7 all-gather.5.cloned.1.call-update
  84.1 182.8 %all-to-all-done = bf16[64,2,16,1024]{3,2,1,0:T(8,128)(2,1)} async-done(((bf16[64,2,16,1024]{3,2,1,0:T(8,128)(2,1)}), bf16[64,2,16,1024]{3,2,1,0:T(8,128)(2,1)}, u32[]{:S(2)}, u32[]{:S(2)}) %all-to-all-start) | async-done | bytes 4194336 | tf_op jit(solution)/shard_map/all_to_all | solution.py:30
  266.9 2.6 copy.27
  269.6 2.0 copy-done.1
  271.5 0.2 fusion.7
  271.8 6.1 %multiply_reduce_fusion = (f32[2]{0:T(128)S(1)}, f32[2,128,1024]{2,1,0:T(8,128)S(1)}) fusion(bf16[2,1024,1024]{2,1,0:T(8,128)(2,1)} %all-gather.5.cloned.1.call-done, bf16[2,1024,1024]{2,1,0:T(8,128)(2,1)} %bitcast.30, bf16[2,1024,128]{2,1,0:T(8,128)(2,1)S(1)} %copy-done), kind=kOutput, calls=%fused_computation.18 | convolution fusion | flops 1074528256 | bytes 9961480 | tf_op jit(solution)/shard_map/snk,skj->snj/dot_general | solution.py:55
  277.9 19.3 %all-reduce = (f32[2]{0:T(128)S(1)}, f32[2]{0:T(128)S(1)}) all-reduce(f32[2]{0:T(128)S(1)} %fusion.7, f32[2]{0:T(128)S(1)} %get-tuple-element.5), channel_id=1, replica_groups=mesh['fsdp'=64,'tensor'=8] {'tensor'}, use_global_device_ids=true, to_apply=%region_3.4 | all-reduce | flops 4 | bytes 32 | tf_op jit(solution)/shard_map/psum | solution.py:63
  297.2 0.2 fusion.8
  297.3 0.3 copy.29
  297.6 0.8 copy.30
  298.5 5.7 %all-to-all-start.1 = ((bf16[2,64,16,128]{3,2,0,1:T(8,128)(2,1)}), bf16[2,64,16,128]{3,2,0,1:T(8,128)(2,1)S(1)}, u32[]{:S(2)}, u32[]{:S(2)}) async-start(bf16[2,64,16,128]{3,2,0,1:T(8,128)(2,1)} %copy.30), calls=%async_computation.1 | async-start | bytes 1048576 | tf_op jit(solution)/shard_map/all_to_all | solution.py:67
  304.2 4.3 %fusion.5 = bf16[2,128,1024]{2,1,0:T(8,128)(2,1)} fusion(bf16[2,128,1024]{2,1,0:T(8,128)(2,1)S(1)} %copy-done.3, bf16[2,1024,1024]{2,1,0:T(8,128)(2,1)} %bitcast.31, s32[]{:T(128)S(6)} %select_n.34, pred[2]{0:T(512)(128)(4,1)S(1)} %dynamic-slice_bitcast_fusion), kind=kOutput, calls=%fused_computation.13 | convolution fusion | flops 538443776 | bytes 5767174 | tf_op jit(solution)/shard_map/skr,skc->src/dot_general | solution.py:41
  308.5 2.4 fusion.4
  310.9 22.2 %all-to-all-done.1 = bf16[2,64,16,128]{3,2,0,1:T(8,128)(2,1)S(1)} async-done(((bf16[2,64,16,128]{3,2,0,1:T(8,128)(2,1)}), bf16[2,64,16,128]{3,2,0,1:T(8,128)(2,1)S(1)}, u32[]{:S(2)}, u32[]{:S(2)}) %all-to-all-start.1) | async-done | bytes 524320 | tf_op jit(solution)/shard_map/all_to_all | solution.py:67
  333.1 1.3 gather_fusion.1
  (22 shorter events, 0.2 us)
Async XLA Ops:
  7.2 264.6 %copy-start = (bf16[2,1024,128]{2,1,0:T(8,128)(2,1)S(1)}, bf16[2,1024,128]{2,1,0:T(8,128)(2,1)}, u32[]{:S(2)}) copy-start(bf16[2,1024,128]{2,1,0:T(8,128)(2,1)} %param.11) | copy-start | bytes 1572868
  7.2 44.2 %all-gather.3.cloned.1.call-start = ((), (), s32[]{:S(2)}) async-start(), calls=%async_computation.2 | async-start | bytes 2359296 | tf_op jit(solution)/shard_map/all_gather | solution.py:26
  67.7 199.2 %all-to-all-start = ((bf16[64,2,16,1024]{3,2,1,0:T(8,128)(2,1)}), bf16[64,2,16,1024]{3,2,1,0:T(8,128)(2,1)}, u32[]{:S(2)}, u32[]{:S(2)}) async-start(bf16[64,2,16,1024]{3,2,1,0:T(8,128)(2,1)} %multiply_convert_fusion), calls=%async_computation | async-start | bytes 8388608 | tf_op jit(solution)/shard_map/all_to_all | solution.py:30
  83.4 188.4 %all-gather.5.cloned.1.call-start = ((), (), s32[]{:S(2)}) async-start(), calls=%async_computation.3 | async-start | bytes 4718592 | tf_op jit(solution)/shard_map/all_gather | solution.py:57
  269.6 2.0 copy-start.1
  277.9 26.3 %copy-start.5 = (s32[64]{0:T(128)S(1)}, s32[64]{0:T(128)}, u32[]{:S(2)}) copy-start(s32[64]{0:T(128)} %param.7) | copy-start | bytes 772
  277.9 26.3 %copy-start.3 = (bf16[2,128,1024]{2,1,0:T(8,128)(2,1)S(1)}, bf16[2,128,1024]{2,1,0:T(8,128)(2,1)}, u32[]{:S(2)}) copy-start(bf16[2,128,1024]{2,1,0:T(8,128)(2,1)} %param.9) | copy-start | bytes 1572868
  298.5 10.1 %copy-start.4 = (bf16[2,128,1024]{2,1,0:T(8,128)(2,1)S(1)}, bf16[2,128,1024]{2,1,0:T(8,128)(2,1)}, u32[]{:S(2)}) copy-start(bf16[2,128,1024]{2,1,0:T(8,128)(2,1)} %param.8) | copy-start | bytes 1572868
  298.5 34.6 %all-to-all-start.1 = ((bf16[2,64,16,128]{3,2,0,1:T(8,128)(2,1)}), bf16[2,64,16,128]{3,2,0,1:T(8,128)(2,1)S(1)}, u32[]{:S(2)}, u32[]{:S(2)}) async-start(bf16[2,64,16,128]{3,2,0,1:T(8,128)(2,1)} %copy.30), calls=%async_computation.1 | async-start | bytes 1048576 | tf_op jit(solution)/shard_map/all_to_all | solution.py:67
  304.2 4.4 %copy-start.2 = (bf16[64,2,16,1024]{3,2,0,1:T(8,128)(2,1)S(1)}, bf16[64,2,16,1024]{3,2,0,1:T(8,128)(2,1)}, u32[]{:S(2)}) copy-start(bf16[64,2,16,1024]{3,2,0,1:T(8,128)(2,1)} %copy-done.1) | copy-start | bytes 12582916
Sparse Core Ops, SparseCore 0:
  10.7 40.6 all-gather.2
  86.3 40.4 all-gather.4
where the time goes:
time: 345 us; the launch traced here: 341 us
  waiting for transfers between devices  246 us (71%)
  starting transfers between devices  21.4 us (6%)
  blocking collectives  19.3 us (6%)
  between operations  14.2 us (4%)
  local copies, waits for them, and re-layouts  13.7 us (4%)
  other arithmetic  13.7 us (4%)
  matrix products  12.8 us (4%)
    all_to_all x1, waiting for transfers between devices, on_device(): lax.all_to_all(picked.reshape(fsdp_count, slot_count, row_share, wide_row...  183 us
    all_gather x1, waiting for transfers between devices, on_device(): lax.all_gather(grads.astype(jnp.bfloat16), 'tensor', axis=2, tiled=True)  40.6 us
    all_to_all x1, waiting for transfers between devices, on_device(): lax.all_to_all(send_back, 'fsdp', split_axis=1, concat_axis=0, tiled=True)  22.2 us
    psum x1, blocking collectives, on_device(): grad_sq, dir_sq = lax.psum((grad_part, dir_part), 'tensor')  19.3 us
    all_to_all x1, starting transfers between devices, on_device(): lax.all_to_all(picked.reshape(fsdp_count, slot_count, row_share, wide_row...  15.6 us
  transfers between devices with their start and end apart: 4, of which 3 were waited for; matrix products, arithmetic and copies ran while one was open for 3% of the time, Pallas kernels for 0%

commit v1 on v0

--- a/solution.py
+++ b/solution.py
@@ -16,29 +16,29 @@
     left_rows = stat_left.shape[1]
     slot_total = fsdp_count * slot_count
     slot_ids = jnp.arange(slot_total, dtype=jnp.int32)
-    block_ids = jnp.arange(block_count, dtype=jnp.int32)
     slot_match = block_slot[None, :] == slot_ids[:, None]
-    block_of_slot = jnp.sum(jnp.where(slot_match, block_ids[None, :], 0), axis=1)
     slot_used = jnp.any(slot_match, axis=1)
     mine_used = lax.dynamic_index_in_dim(
         slot_used.reshape(fsdp_count, slot_count), owner_index, 0, keepdims=False
     )
-    wide_rows = lax.all_gather(grads.astype(jnp.bfloat16), "tensor", axis=2, tiled=True).astype(
-        grads.dtype
-    )
-    picked = wide_rows[block_of_slot] * slot_used[:, None, None].astype(wide_rows.dtype)
-    arrived = lax.all_to_all(
-        picked.reshape(fsdp_count, slot_count, row_share, wide_rows.shape[2]).astype(jnp.bfloat16),
+    whole_root_left = lax.all_gather(root_left, "tensor", axis=1, tiled=True)
+    picked = jnp.einsum(
+        "sb,brc->src",
+        slot_match.astype(jnp.bfloat16),
+        grads.astype(jnp.bfloat16),
+        preferred_element_type=jnp.float32,
+    ).astype(jnp.bfloat16)
+    col_slab = lax.all_to_all(
+        picked.reshape(fsdp_count, slot_count, row_share, col_share),
         "fsdp",
         split_axis=0,
         concat_axis=2,
         tiled=True,
-    ).astype(jnp.float32)
-    full_block = arrived[0]
-    col_slab = lax.dynamic_slice_in_dim(full_block, tensor_index * col_share, col_share, 2)
+    )[0]
+    full_block = lax.all_gather(col_slab, "tensor", axis=2, tiled=True)
     row_block = lax.dynamic_slice_in_dim(full_block, tensor_index * left_rows, left_rows, 1)
-    left_prod = jnp.einsum("srk,sck->src", row_block, full_block, precision=lax.Precision.HIGHEST)
-    right_prod = jnp.einsum("skr,skc->src", col_slab, full_block, precision=lax.Precision.HIGHEST)
+    left_prod = jnp.einsum("srk,sck->src", row_block, full_block, preferred_element_type=jnp.float32)
+    right_prod = jnp.einsum("skr,skc->src", col_slab, full_block, preferred_element_type=jnp.float32)
     keep_mask = mine_used[:, None, None]
     left_old = stat_left.astype(jnp.float32)
     right_old = stat_right.astype(jnp.float32)
@@ -48,18 +48,15 @@
     new_right = jnp.where(
         keep_mask, stat_decay * right_old + (1.0 - stat_decay) * right_prod, right_old
     ).astype(jnp.bfloat16)
-    grad_half = full_block.astype(jnp.bfloat16)
     half_right = jnp.einsum(
-        "sik,skj->sij", grad_half, root_right, preferred_element_type=jnp.float32
+        "sik,skj->sij", full_block, root_right, preferred_element_type=jnp.float32
     ).astype(jnp.bfloat16)
     precond = jnp.einsum(
-        "snk,skj->snj",
-        lax.all_gather(root_left, "tensor", axis=1, tiled=True),
-        half_right,
-        preferred_element_type=jnp.float32,
+        "snk,skj->snj", whole_root_left, half_right, preferred_element_type=jnp.float32
     )
+    slab_wide = col_slab.astype(jnp.float32)
     dir_part = jnp.sum(precond * precond, axis=(1, 2))
-    grad_part = jnp.sum(col_slab * col_slab, axis=(1, 2))
+    grad_part = jnp.sum(slab_wide * slab_wide, axis=(1, 2))
     grad_sq, dir_sq = lax.psum((grad_part, dir_part), "tensor")
     graft_scale = jnp.sqrt(grad_sq / (dir_sq + graft_eps))
     direction = (precond * graft_scale[:, None, None]).astype(jnp.bfloat16)

time: 345 us -> 178 us (0.52)
  the two profiles are of different devices: /device:TPU:1 before, /device:TPU:8 now
where the time goes in v1:
time: 178 us; the launch traced here: 177 us
  blocking collectives  65.7 us (37%)
  waiting for transfers between devices  61.4 us (34%)
  starting transfers between devices  15.8 us (9%)
  between operations  14.2 us (8%)
  matrix products  14 us (8%)
  local copies, waits for them, and re-layouts  3.9 us (2%)
  other arithmetic  2.54 us (1%)
    all_to_all x1, blocking collectives, on_device(): lax.all_to_all(picked.reshape(fsdp_count, slot_count, row_share, col_shar...  51.2 us
    all_gather x1, waiting for transfers between devices, on_device(): full_block = lax.all_gather(col_slab, 'tensor', axis=2, tiled=True)  37 us
    all_to_all x1, waiting for transfers between devices, on_device(): lax.all_to_all(send_back, 'fsdp', split_axis=1, concat_axis=0, tiled=True)  23.7 us
    all_to_all x1, starting transfers between devices, on_device(): lax.all_to_all(send_back, 'fsdp', split_axis=1, concat_axis=0, tiled=True)  15.7 us
    psum x1, blocking collectives, on_device(): grad_sq, dir_sq = lax.psum((grad_part, dir_part), 'tensor')  14.4 us
    dot_general x1, matrix products, on_device(): jnp.einsum('snk,skj->snj', whole_root_left, half_right, preferred_element...  6.15 us
    dot_general x1, matrix products, on_device(): jnp.einsum('srk,sck->src', row_block, full_block, preferred_element_type=...  4.9 us
  transfers between devices with their start and end apart: 3, of which 2 were waited for; matrix products, arithmetic and copies ran while one was open for 7% of the time, Pallas kernels for 0%

profile of v1, /device:TPU:8, one launch (start us, length us, event | category | flops | bytes accessed | tf_op | source)
XLA Modules:
  0.0 177.5 jit_solution(267170964903311837)
XLA Ops:
  7.2 0.0 all-gather.5.cloned.1.call-start
  7.2 0.7 all-gather.5.cloned.1.call-update
  7.9 0.0 all-gather.3.cloned.1.call-start
  8.0 1.1 convert_element_type.32
  9.0 1.1 convolution_convert_fusion.1
  10.1 0.4 copy.18
  10.5 51.2 %all_to_all.30 = bf16[64,2,16,128]{3,1,2,0:T(2,128)(2,1)S(1)} all-to-all(bf16[64,2,16,128]{3,1,2,0:T(2,128)(2,1)S(1)} %copy.18), channel_id=1, replica_groups=mesh['fsdp'=64,'tensor'=8] {'fsdp'}, dimensions={0} | all-to-all | bytes 1048576 | tf_op jit(solution)/shard_map/all_to_all | solution.py:31
  61.7 0.9 copy.19
  62.6 0.0 all-gather.3.cloned.1.call-update
  62.6 1.2 multiply_reduce_fusion.1
  63.8 0.0 all-gather.5.cloned.1.call-done
  63.8 37.0 %all-gather.3.cloned.1.call-done = bf16[2,1024,1024]{2,1,0:T(8,128)(2,1)} async-done(((bf16[2,1024,128]{2,1,0:T(8,128)(2,1)}), bf16[2,1024,1024]{2,1,0:T(8,128)(2,1)}) %all-gather.3.cloned.1.call-update) | async-done | bytes 4194320 | tf_op jit(solution)/shard_map/all_gather | solution.py:38
  100.8 6.2 %multiply_reduce_fusion = (f32[2]{0:T(128)S(1)}, f32[2,128,1024]{2,1,0:T(8,128)S(1)}) fusion(bf16[2,1024,1024]{2,1,0:T(8,128)(2,1)} %all-gather.5.cloned.1.call-done, bf16[2,1024,1024]{2,1,0:T(8,128)(2,1)} %all-gather.3.cloned.1.call-done, bf16[2,1024,128]{2,1,0:T(8,128)(2,1)S(1)} %copy-done), kind=kOutput, calls=%fused_computation.15 | convolution fusion | flops 1074528256 | bytes 9961480 | tf_op jit(solution)/shard_map/snk,skj->snj/dot_general | solution.py:54
  107.0 14.4 %all-reduce = (f32[2]{0:T(128)S(1)}, f32[2]{0:T(128)S(1)}) all-reduce(f32[2]{0:T(128)S(1)} %multiply_reduce_fusion.1, f32[2]{0:T(128)S(1)} %get-tuple-element.5), channel_id=1, replica_groups=mesh['fsdp'=64,'tensor'=8] {'tensor'}, use_global_device_ids=true, to_apply=%region_1.2 | all-reduce | flops 4 | bytes 32 | tf_op jit(solution)/shard_map/psum | solution.py:60
  121.4 0.2 fusion.7
  121.6 0.3 copy.21
  121.9 0.9 copy.22
  122.7 15.7 %all-to-all-start.1 = ((bf16[2,64,16,128]{3,2,0,1:T(8,128)(2,1)}), bf16[2,64,16,128]{3,2,0,1:T(8,128)(2,1)S(1)}, u32[]{:S(2)}, u32[]{:S(2)}) async-start(bf16[2,64,16,128]{3,2,0,1:T(8,128)(2,1)} %copy.22), calls=%async_computation.1 | async-start | bytes 1048576 | tf_op jit(solution)/shard_map/all_to_all | solution.py:64
  138.5 0.1 fusion.10
  138.6 0.2 reshape.27
  138.8 4.9 %fusion.4 = bf16[2,128,1024]{2,1,0:T(8,128)(2,1)} fusion(bf16[2,128,1024]{2,1,0:T(8,128)(2,1)S(1)} %copy-done.4, bf16[2,1024,1024]{2,1,0:T(8,128)(2,1)} %all-gather.3.cloned.1.call-done, s32[]{:T(128)S(6)} %select_n.19, pred[2]{0:T(512)(128)(4,1)S(1)} %dynamic-slice_bitcast_fusion), kind=kOutput, calls=%fused_computation.10 | convolution fusion | flops 538443776 | bytes 5767174 | tf_op jit(solution)/shard_map/srk,sck->src/dot_general | solution.py:40
  143.7 1.8 %fusion.5 = bf16[2,128,1024]{2,1,0:T(8,128)(2,1)} fusion(bf16[2,128,1024]{2,1,0:T(8,128)(2,1)S(1)} %copy-done.5, bf16[2,1024,128]{2,1,0:T(8,128)(2,1)S(1)} %bitcast.27, bf16[2,1024,1024]{2,1,0:T(8,128)(2,1)S(1)} %copy-done.3, pred[2]{0:T(512)(128)(4,1)S(1)} %dynamic-slice_bitcast_fusion), kind=kOutput, calls=%fused_computation.11 | convolution fusion | flops 538443776 | bytes 5767170 | tf_op jit(solution)/shard_map/skr,skc->src/dot_general | solution.py:41
  145.6 23.7 %all-to-all-done.1 = bf16[2,64,16,128]{3,2,0,1:T(8,128)(2,1)S(1)} async-done(((bf16[2,64,16,128]{3,2,0,1:T(8,128)(2,1)}), bf16[2,64,16,128]{3,2,0,1:T(8,128)(2,1)S(1)}, u32[]{:S(2)}, u32[]{:S(2)}) %all-to-all-start.1) | async-done | bytes 524320 | tf_op jit(solution)/shard_map/all_to_all | solution.py:64
  169.3 1.3 gather_fusion
  (16 shorter events, 0.1 us)
Async XLA Ops:
  7.2 93.6 %copy-start = (bf16[2,1024,128]{2,1,0:T(8,128)(2,1)S(1)}, bf16[2,1024,128]{2,1,0:T(8,128)(2,1)}, u32[]{:S(2)}) copy-start(bf16[2,1024,128]{2,1,0:T(8,128)(2,1)} %param.11) | copy-start | bytes 1572868
  7.2 56.6 %all-gather.5.cloned.1.call-start = ((), (), s32[]{:S(2)}) async-start(), calls=%async_computation.3 | async-start | bytes 4718592 | tf_op jit(solution)/shard_map/all_gather | solution.py:24
  7.9 92.9 %all-gather.3.cloned.1.call-start = ((), (), s32[]{:S(2)}) async-start(), calls=%async_computation.2 | async-start | bytes 4718592 | tf_op jit(solution)/shard_map/all_gather | solution.py:38
  107.0 31.6 %copy-start.2 = (s32[64]{0:T(128)S(1)}, s32[64]{0:T(128)}, u32[]{:S(2)}) copy-start(s32[64]{0:T(128)} %param.7) | copy-start | bytes 772
  107.0 31.9 %copy-start.4 = (bf16[2,128,1024]{2,1,0:T(8,128)(2,1)S(1)}, bf16[2,128,1024]{2,1,0:T(8,128)(2,1)}, u32[]{:S(2)}) copy-start(bf16[2,128,1024]{2,1,0:T(8,128)(2,1)} %param.8) | copy-start | bytes 1572868
  121.6 22.2 %copy-start.1 = (bf16[1,2,64,16,128]{4,3,2,1,0:T(8,128)(2,1)S(1)}, bf16[1,2,64,16,128]{4,3,2,1,0:T(8,128)(2,1)}, u32[]{:S(2)}) copy-start(bf16[1,2,64,16,128]{4,3,2,1,0:T(8,128)(2,1)} %copy.19) | copy-start | bytes 1572868
  121.6 22.2 %copy-start.5 = (bf16[2,128,1024]{2,1,0:T(8,128)(2,1)S(1)}, bf16[2,128,1024]{2,1,0:T(8,128)(2,1)}, u32[]{:S(2)}) copy-start(bf16[2,128,1024]{2,1,0:T(8,128)(2,1)} %param.9) | copy-start | bytes 1572868
  122.7 46.6 %all-to-all-start.1 = ((bf16[2,64,16,128]{3,2,0,1:T(8,128)(2,1)}), bf16[2,64,16,128]{3,2,0,1:T(8,128)(2,1)S(1)}, u32[]{:S(2)}, u32[]{:S(2)}) async-start(bf16[2,64,16,128]{3,2,0,1:T(8,128)(2,1)} %copy.22), calls=%async_computation.1 | async-start | bytes 1048576 | tf_op jit(solution)/shard_map/all_to_all | solution.py:64
  138.8 5.0 %copy-start.3 = (bf16[2,1024,1024]{2,1,0:T(8,128)(2,1)S(1)}, bf16[2,1024,1024]{2,1,0:T(8,128)(2,1)}, u32[]{:S(2)}) copy-start(bf16[2,1024,1024]{2,1,0:T(8,128)(2,1)} %all-gather.3.cloned.1.call-done) | copy-start | bytes 12582916
Sparse Core Ops, SparseCore 0:
  10.1 44.1 all-gather.4
  62.7 38.0 all-gather.2

commit v2 on v1

v2 whole, which is shorter than its diff:
```python
import functools

import jax
import jax.numpy as jnp
from jax import lax
from jax.experimental import pallas as pl
from jax.experimental.pallas import tpu as pltpu
from jax.sharding import PartitionSpec as P

stat_decay = 0.95
graft_eps = 1e-06
Y_CHIPS = 4
TILE = 256


def kernel(
    owners,
    peers,
    code,
    block_slot,
    grads,
    stat_left,
    stat_right,
    root_left,
    root_right,
    directions,
    new_left,
    new_right,
    g_full,
    rl_full,
    pick,
    half,
    precond,
    dir_buf,
    back,
    parts,
    a2a_send,
    a2a_recv,
    back_send,
    back_recv,
    part_send,
    part_recv,
    ring_send,
    ring_recv,
):
    slots = stat_left.shape[0]
    blocks, row_share, col_share = grads.shape
    order = g_full.shape[1]
    me = lax.axis_index("fsdp")
    t = lax.axis_index("tensor")
    z_chips = owners // Y_CHIPS
    my_z, my_y = me // Y_CHIPS, me % Y_CHIPS
    x, core = t // 2, t % 2
    x_chips = peers // 2
    left = ((x + x_chips - 1) % x_chips) * 2 + core
    right = ((x + 1) % x_chips) * 2 + core
    across = ((x + 2) % x_chips) * 2 + core
    sibling = x * 2 + 1 - core

    def partner(k):
        j, dy = k // Y_CHIPS, k % Y_CHIPS
        hop = (j + 1) // 2
        dz = jnp.where(j % 2 == 1, hop, z_chips - hop)
        return ((my_z + dz) % z_chips) * Y_CHIPS + (my_y + dy) % Y_CHIPS

    def to_owner(f):
        return {"fsdp": f, "tensor": t}

    def to_peer(u):
        return {"fsdp": me, "tensor": u}

    barrier = pltpu.get_barrier_semaphore()

    def greet_owner(k, carry):
        pl.semaphore_signal(barrier, inc=1, device_id=to_owner((me + k) % owners))
        return carry

    def greet_peer(k, carry):
        pl.semaphore_signal(barrier, inc=1, device_id=to_peer((t + k) % peers))
        return carry

    lax.fori_loop(1, owners, greet_owner, 0)
    lax.fori_loop(1, peers, greet_peer, 0)
    pl.semaphore_wait(barrier, owners + peers - 2)

    def g_part(s):
        def view(u, part=None):
            cols = pl.ds(pl.multiple_of(u * col_share, col_share), col_share)
            if part is None:
                return g_full.at[s, :, cols]
            return g_full.at[s, pl.ds(part * (order // 2), order // 2), cols]

        return view

    rl_rows = root_left.shape[1]

    def rl_part(s):
        def view(u, part=None):
            if part is None:
                return rl_full.at[s, pl.ds(pl.multiple_of(u * rl_rows, rl_rows), rl_rows)]
            size = rl_rows // 2
            return rl_full.at[s, pl.ds(pl.multiple_of(u * rl_rows + part * size, size), size)]

        return view

    def push(ring, n, piece, u):
        pltpu.make_async_remote_copy(
            src_ref=piece,
            dst_ref=piece,
            send_sem=ring_send.at[ring],
            recv_sem=ring_recv.at[ring, n],
            device_id=to_peer(u),
        ).start()

    def arrive(ring, n, piece):
        pltpu.make_async_copy(piece, piece, ring_recv.at[ring, n]).wait()

    def ring_begin(ring, view):
        push(ring, 0, view(t), right)
        push(ring, 1, view(t), left)
        push(ring, 4, view(t), sibling)

    def ring_forward(ring, view):
        arrive(ring, 0, view(left))
        push(ring, 2, view(left, 0), right)
        push(ring, 5, view(left), sibling)
        arrive(ring, 1, view(right))
        push(ring, 3, view(right, 1), left)
        push(ring, 6, view(right), sibling)

    def ring_last(ring, view):
        arrive(ring, 2, view(across, 0))
        arrive(ring, 3, view(across, 1))
        push(ring, 7, view(across), sibling)

    def ring_end(ring, view):
        for n, u in ((4, t), (5, left), (6, right), (7, across)):
            arrive(ring, n, view(u // 2 * 2 + 1 - core))

    my_rows = pl.ds(pl.multiple_of(t * rl_rows, rl_rows), rl_rows)
    for s in range(slots):
        rl_full[s, my_rows, :] = root_left[s]
        ring_begin(s, rl_part(s))

    g_rows = pl.ds(pl.multiple_of(me * row_share, row_share), row_share)
    g_cols = pl.ds(pl.multiple_of(t * col_share, col_share), col_share)

    for s in range(slots):

        def give(k, carry, s=s):
            f = partner(k)
            pick[s, f] = grads[code[slots * f + s] // 2].astype(pick.dtype)
            pltpu.make_async_remote_copy(
                src_ref=pick.at[s, f],
                dst_ref=g_full.at[s, g_rows, g_cols],
                send_sem=a2a_send.at[s],
                recv_sem=a2a_recv.at[s],
                device_id=to_owner(f),
            ).start()
            return carry

        lax.fori_loop(1, owners, give, 0)
        g_full[s, g_rows, g_cols] = grads[code[slots * me + s] // 2].astype(g_full.dtype)

    def owners_but_me(ref, sem):
        whole = ref.at[pl.ds(0, owners - 1)]
        pltpu.make_async_copy(whole, whole, sem).wait()

    for s in range(slots):
        ring_forward(s, rl_part(s))

    def preconditioned(s):
        def half_tile(i, carry):
            rows = pl.ds(pl.multiple_of(i * TILE, TILE), TILE)
            half[s, rows, :] = jnp.dot(
                g_full[s, rows, :], root_right[s], preferred_element_type=jnp.float32
            ).astype(half.dtype)
            return carry

        lax.fori_loop(0, order // TILE, half_tile, 0)

        def squares(tile):
            return jnp.sum((tile * tile).reshape(-1, 8, col_share), axis=0)

        def precond_tile(i, carry):
            dir_sum, grad_sum = carry
            rows = pl.ds(pl.multiple_of(i * TILE, TILE), TILE)
            tile = jnp.dot(rl_full[s, rows, :], half[s], preferred_element_type=jnp.float32)
            precond[s, rows, :] = tile
            grad = g_full[s, rows, g_cols].astype(jnp.float32)
            return dir_sum + squares(tile), grad_sum + squares(grad)

        zero = jnp.zeros((8, col_share), jnp.float32)
        dir_sum, grad_sum = lax.fori_loop(0, order // TILE, precond_tile, (zero, zero))
        parts[s, t, 0:8] = dir_sum
        parts[s, t, 8:16] = grad_sum

        def tell(k, carry):
            pltpu.make_async_remote_copy(
                src_ref=parts.at[s, t],
                dst_ref=parts.at[s, t],
                send_sem=part_send.at[s],
                recv_sem=part_recv.at[s],
                device_id=to_peer((t + k) % peers),
            ).start()
            return carry

        lax.fori_loop(1, peers, tell, 0)

    def peers_but_me(s, sem):
        whole = parts.at[s, pl.ds(0, peers - 1)]
        pltpu.make_async_copy(whole, whole, sem).wait()

    def send_back(s):
        peers_but_me(s, part_recv.at[s])
        total = jnp.sum(parts[s], axis=0)
        dir_sq = jnp.sum(total[0:8], keepdims=True)
        grad_sq = jnp.sum(total[8:16], keepdims=True)
        scale = jnp.sqrt(grad_sq / (dir_sq + graft_eps))

        def scaled(i, carry):
            rows = pl.ds(pl.multiple_of(i * TILE, TILE), TILE)
            dir_buf[s, rows, :] = (precond[s, rows, :] * scale).astype(dir_buf.dtype)
            return carry

        lax.fori_loop(0, order // TILE, scaled, 0)

        def give(k, carry):
            f = partner(k)
            rows = pl.ds(pl.multiple_of(f * row_share, row_share), row_share)
            pltpu.make_async_remote_copy(
                src_ref=dir_buf.at[s, rows],
                dst_ref=back.at[slots * me + s],
                send_sem=back_send.at[s],
                recv_sem=back_recv.at[s],
                device_id=to_owner(f),
            ).start()
            return carry

        lax.fori_loop(1, owners, give, 0)
        back[slots * me + s] = dir_buf[s, g_rows]

    def statistics(s):
        used = code[slots * me + s] % 2 == 1

        def left_tile(i, carry):
            cols = pl.ds(pl.multiple_of(i * TILE, TILE), TILE)
            prod = lax.dot_general(
                g_full[s, my_rows, :],
                g_full[s, cols, :],
                (((1,), (1,)), ((), ())),
                preferred_element_type=jnp.float32,
            )
            old = stat_left[s, :, cols].astype(jnp.float32)
            new = jnp.where(used, stat_decay * old + (1.0 - stat_decay) * prod, old)
            new_left[s, :, cols] = new.astype(new_left.dtype)
            return carry

        def right_tile(i, carry):
            cols = pl.ds(pl.multiple_of(i * TILE, TILE), TILE)
            prod = lax.dot_general(
                g_full[s, :, g_cols],
                g_full[s, :, cols],
                (((0,), (0,)), ((), ())),
                preferred_element_type=jnp.float32,
            )
            old = stat_right[s, :, cols].astype(jnp.float32)
            new = jnp.where(used, stat_decay * old + (1.0 - stat_decay) * prod, old)
            new_right[s, :, cols] = new.astype(new_right.dtype)
            return carry

        lax.fori_loop(0, order // TILE, left_tile, 0)
        lax.fori_loop(0, order // TILE, right_tile, 0)

    owners_but_me(pick.at[0], a2a_recv.at[0])
    ring_begin(slots, g_part(0))
    for s in range(slots):
        ring_last(s, rl_part(s))
    ring_forward(slots, g_part(0))
    ring_end(0, rl_part(0))
    ring_last(slots, g_part(0))
    owners_but_me(pick.at[1], a2a_recv.at[1])
    ring_begin(slots + 1, g_part(1))
    ring_end(slots, g_part(0))
    preconditioned(0)
    ring_forward(slots + 1, g_part(1))
    send_back(0)
    ring_end(1, rl_part(1))
    ring_last(slots + 1, g_part(1))
    ring_end(slots + 1, g_part(1))
    preconditioned(1)
    send_back(1)
    statistics(0)
    statistics(1)

    for s in range(slots):
        owners_but_me(back, back_recv.at[s])

    def choose(b, carry):
        directions[b] = back[block_slot[b]]
        return carry

    lax.fori_loop(0, blocks, choose, 0)

    for s in range(slots):
        owners_but_me(pick.at[s], a2a_send.at[s])
        owners_but_me(back, back_send.at[s])
        peers_but_me(s, part_send.at[s])
        for ring in (s, slots + s):
            sent = rl_full.at[s, pl.ds(0, 7 * rl_rows)]
            pltpu.make_async_copy(sent, sent, ring_send.at[ring]).wait()


def on_device(grads, block_slot, stat_left, stat_right, root_left, root_right):
    owners = lax.axis_size("fsdp")
    peers = lax.axis_size("tensor")
    blocks, row_share, col_share = grads.shape
    slots, left_rows, order = stat_left.shape
    slot_ids = jnp.arange(owners * slots, dtype=jnp.int32)
    block_ids = jnp.arange(blocks, dtype=jnp.int32)
    match = block_slot[None, :] == slot_ids[:, None]
    code = jnp.sum(jnp.where(match, 2 * block_ids[None, :] + 1, 0), axis=1, dtype=jnp.int32)
    smem = pl.BlockSpec(memory_space=pltpu.SMEM)
    vmem = pl.BlockSpec(memory_space=pltpu.VMEM)
    bf16 = jnp.bfloat16
    dma = pltpu.SemaphoreType.DMA
    return pl.pallas_call(
        functools.partial(kernel, owners, peers),
        out_shape=(
            jax.ShapeDtypeStruct(grads.shape, bf16),
            jax.ShapeDtypeStruct(stat_left.shape, bf16),
            jax.ShapeDtypeStruct(stat_right.shape, bf16),
        ),
        in_specs=[smem, smem] + [vmem] * 5,
        out_specs=(vmem, vmem, vmem),
        scratch_shapes=[
            pltpu.VMEM((slots, order, order), bf16),
            pltpu.VMEM((slots, order, order), bf16),
            pltpu.VMEM((slots, owners, row_share, col_share), bf16),
            pltpu.VMEM((slots, order, col_share), bf16),
            pltpu.VMEM((slots, order, col_share), jnp.float32),
            pltpu.VMEM((slots, order, col_share), bf16),
            pltpu.VMEM((slots * owners, row_share, col_share), bf16),
            pltpu.VMEM((slots, peers, 16, col_share), jnp.float32),
            dma((slots,)),
            dma((slots,)),
            dma((slots,)),
            dma((slots,)),
            dma((slots,)),
            dma((slots,)),
            dma((2 * slots,)),
            dma((2 * slots, 8)),
        ],
        compiler_params=pltpu.CompilerParams(
            collective_id=0, has_side_effects=True, vmem_limit_bytes=48 * 1024 * 1024
        ),
        name="shampoo_step",
    )(code, block_slot, grads, stat_left, stat_right, root_left, root_right)


def solution(mesh):
    placed = (
        P(None, "fsdp", "tensor"),
        P(),
        P("fsdp", "tensor", None),
        P("fsdp", "tensor", None),
        P("fsdp", "tensor", None),
        P("fsdp", None, "tensor"),
    )
    return jax.shard_map(
        on_device,
        mesh=mesh,
        in_specs=placed,
        out_specs=(P(None, "fsdp", "tensor"), P("fsdp", "tensor", None), P("fsdp", "tensor", None)),
        check_vma=False,
    )
```

time: 178 us -> 99.2 us (0.56)
  the two profiles are of different devices: /device:TPU:8 before, /device:TPU:1 now
where the time goes in v2:
time: 99.2 us; the launch traced here: 98.8 us
  Pallas kernels  89.9 us (91%)
  local copies, waits for them, and re-layouts  8.13 us (8%)
    pallas_call x1, Pallas kernels, on_device(): pl.pallas_call(functools.partial(kernel, owners, peers), out_shape=(jax.S...  89.9 us
    unnamed x15, local copies, waits for them, and re-layouts  8.13 us

profile of v2, /device:TPU:1, one launch (start us, length us, event | category | flops | bytes accessed | tf_op | source)
XLA Modules:
  0.0 98.8 jit_solution(18348539211842849435)
XLA Ops:
  0.6 0.0 copy-start.5
  0.7 0.6 copy-done.5
  1.3 0.1 select_reduce_fusion.code
  1.4 0.0 copy-start
  1.4 1.0 %copy-done = f32[64,16,128]{2,1,0:T(8,128)S(1)} copy-done((f32[64,16,128]{2,1,0:T(8,128)S(1)}, f32[64,16,128]{2,1,0:T(8,128)}, u32[]{:S(2)}) %copy-start) | copy-done | bytes 524312
  2.4 0.0 copy-start.1
  2.4 1.0 %copy-done.1 = bf16[2,128,1024]{2,1,0:T(8,128)(2,1)S(1)} copy-done((bf16[2,128,1024]{2,1,0:T(8,128)(2,1)S(1)}, bf16[2,128,1024]{2,1,0:T(8,128)(2,1)}, u32[]{:S(2)}) %copy-start.1) | copy-done | bytes 524312
  3.5 0.0 copy-start.2
  3.5 1.0 %copy-done.2 = bf16[2,128,1024]{2,1,0:T(8,128)(2,1)S(1)} copy-done((bf16[2,128,1024]{2,1,0:T(8,128)(2,1)S(1)}, bf16[2,128,1024]{2,1,0:T(8,128)(2,1)}, u32[]{:S(2)}) %copy-start.2) | copy-done | bytes 524312
  4.5 0.0 copy-start.3
  4.5 1.0 %copy-done.3 = bf16[2,128,1024]{2,1,0:T(8,128)(2,1)S(1)} copy-done((bf16[2,128,1024]{2,1,0:T(8,128)(2,1)S(1)}, bf16[2,128,1024]{2,1,0:T(8,128)(2,1)}, u32[]{:S(2)}) %copy-start.3) | copy-done | bytes 524312
  5.6 0.0 copy-start.4
  5.6 1.0 %copy-done.4 = bf16[2,1024,128]{2,1,0:T(8,128)(2,1)S(1)} copy-done((bf16[2,1024,128]{2,1,0:T(8,128)(2,1)S(1)}, bf16[2,1024,128]{2,1,0:T(8,128)(2,1)}, u32[]{:S(2)}) %copy-start.4) | copy-done | bytes 524312
  6.6 89.9 %shampoo_step.1 = (bf16[64,16,128]{2,1,0:T(8,128)(2,1)S(1)}, bf16[2,128,1024]{2,1,0:T(8,128)(2,1)S(1)}, bf16[2,128,1024]{2,1,0:T(8,128)(2,1)S(1)}) custom-call(s32[128]{0:T(128)S(1)} %select_reduce_fusion.code, s32[64]{0:T(128)S(1)} %copy-done.5, f32[64,16,128]{2,1,0:T(8,128)S(1)} %copy-done, bf16[2,128,1024]{2,1,0:T(8,128)(2,1)S(1)} %copy-done.1, ...), custom_call_target="tpu_custom_call" | custom-call | tf_op jit(solution)/shard_map/shampoo_step/pallas_call | solution.py:327
  96.5 0.7 copy.12
  97.2 0.8 copy.13
  98.0 0.8 copy.14
  (1 shorter events, 0.0 us)
Async XLA Ops:
  0.6 0.7 copy-start.5
  1.4 1.0 %copy-start = (f32[64,16,128]{2,1,0:T(8,128)S(1)}, f32[64,16,128]{2,1,0:T(8,128)}, u32[]{:S(2)}) copy-start(f32[64,16,128]{2,1,0:T(8,128)} %grads.1) | copy-start | bytes 1572868
  2.4 1.0 %copy-start.1 = (bf16[2,128,1024]{2,1,0:T(8,128)(2,1)S(1)}, bf16[2,128,1024]{2,1,0:T(8,128)(2,1)}, u32[]{:S(2)}) copy-start(bf16[2,128,1024]{2,1,0:T(8,128)(2,1)} %stat_left.1) | copy-start | bytes 1572868
  3.5 1.0 %copy-start.2 = (bf16[2,128,1024]{2,1,0:T(8,128)(2,1)S(1)}, bf16[2,128,1024]{2,1,0:T(8,128)(2,1)}, u32[]{:S(2)}) copy-start(bf16[2,128,1024]{2,1,0:T(8,128)(2,1)} %stat_right.1) | copy-start | bytes 1572868
  4.5 1.0 %copy-start.3 = (bf16[2,128,1024]{2,1,0:T(8,128)(2,1)S(1)}, bf16[2,128,1024]{2,1,0:T(8,128)(2,1)}, u32[]{:S(2)}) copy-start(bf16[2,128,1024]{2,1,0:T(8,128)(2,1)} %root_left.1) | copy-start | bytes 1572868
  5.6 1.0 %copy-start.4 = (bf16[2,1024,128]{2,1,0:T(8,128)(2,1)S(1)}, bf16[2,1024,128]{2,1,0:T(8,128)(2,1)}, u32[]{:S(2)}) copy-start(bf16[2,1024,128]{2,1,0:T(8,128)(2,1)} %root_right.1) | copy-start | bytes 1572868

commit v3 on v2

v3 whole, which is shorter than its diff:
```python
import functools

import jax
import jax.numpy as jnp
from jax import lax
from jax.experimental import pallas as pl
from jax.experimental.pallas import tpu as pltpu
from jax.sharding import PartitionSpec as P

stat_decay = 0.95
graft_eps = 1e-06
TILE = 256
Y_CHIPS = 4


def kernel(
    owners,
    peers,
    code,
    block_slot,
    grads_hbm,
    stat_left_hbm,
    stat_right_hbm,
    root_left_hbm,
    root_right_hbm,
    directions,
    new_left_hbm,
    new_right_hbm,
    grads,
    stat_left,
    stat_right,
    root_right,
    new_left,
    new_right,
    g_full,
    rl_full,
    pick,
    half,
    dir_buf,
    back,
    parts,
    scales,
    scale_rows,
    a2a_send,
    a2a_recv,
    back_send,
    back_recv,
    part_send,
    part_recv,
    scale_send,
    scale_recv,
    ring_send,
    ring_recv,
    load_sem,
    store_sem,
):
    slots, rl_rows, _ = root_left_hbm.shape
    blocks, row_share, col_share = grads.shape
    order = g_full.shape[1]
    me = lax.axis_index("fsdp")
    t = lax.axis_index("tensor")
    z_chips = owners // Y_CHIPS
    my_z, my_y = me // Y_CHIPS, me % Y_CHIPS
    x, core = t // 2, t % 2
    x_chips = peers // 2
    left = ((x + x_chips - 1) % x_chips) * 2 + core
    right = ((x + 1) % x_chips) * 2 + core
    across = ((x + 2) % x_chips) * 2 + core
    sibling = x * 2 + 1 - core

    def partner(k):
        k = owners - k
        j, dy = k // Y_CHIPS, k % Y_CHIPS
        hop = (j + 1) // 2
        dz = jnp.where(j % 2 == 1, hop, z_chips - hop)
        return ((my_z + dz) % z_chips) * Y_CHIPS + (my_y + dy) % Y_CHIPS

    def to_owner(f):
        return {"fsdp": f, "tensor": t}

    def to_peer(u):
        return {"fsdp": me, "tensor": u}

    my_rows = pl.ds(pl.multiple_of(t * rl_rows, rl_rows), rl_rows)
    g_rows = pl.ds(pl.multiple_of(me * row_share, row_share), row_share)
    g_cols = pl.ds(pl.multiple_of(t * col_share, col_share), col_share)

    loads = [
        pltpu.make_async_copy(source, target, load_sem.at[n])
        for n, (source, target) in enumerate(
            (
                (root_left_hbm, rl_full.at[:, my_rows]),
                (grads_hbm, grads),
                (root_right_hbm, root_right),
                (stat_left_hbm, stat_left),
                (stat_right_hbm, stat_right),
            )
        )
    ]
    for load in loads:
        load.start()

    barrier = pltpu.get_barrier_semaphore()

    def greet_owner(k, carry):
        pl.semaphore_signal(barrier, inc=1, device_id=to_owner((me + k) % owners))
        return carry

    def greet_peer(k, carry):
        pl.semaphore_signal(barrier, inc=1, device_id=to_peer((t + k) % peers))
        return carry

    lax.fori_loop(1, owners, greet_owner, 0)
    lax.fori_loop(1, peers, greet_peer, 0)
    pl.semaphore_wait(barrier, owners + peers - 2)

    def g_part(s):
        def view(u, part=None):
            cols = pl.ds(pl.multiple_of(u * col_share, col_share), col_share)
            if part is None:
                return g_full.at[s, :, cols]
            return g_full.at[s, pl.ds(part * (order // 2), order // 2), cols]

        return view

    def rl_part(s):
        def view(u, part=None):
            if part is None:
                return rl_full.at[s, pl.ds(pl.multiple_of(u * rl_rows, rl_rows), rl_rows)]
            size = rl_rows // 2
            return rl_full.at[s, pl.ds(pl.multiple_of(u * rl_rows + part * size, size), size)]

        return view

    def push(ring, n, piece, u):
        pltpu.make_async_remote_copy(
            src_ref=piece,
            dst_ref=piece,
            send_sem=ring_send.at[ring],
            recv_sem=ring_recv.at[ring, n],
            device_id=to_peer(u),
        ).start()

    def arrive(ring, n, piece):
        pltpu.make_async_copy(piece, piece, ring_recv.at[ring, n]).wait()

    def ring_begin(ring, view):
        push(ring, 0, view(t, 0), right)
        push(ring, 1, view(t, 1), left)
        push(ring, 2, view(t, 1), right)
        push(ring, 3, view(t, 0), left)
        push(ring, 6, view(t), sibling)

    def ring_forward(ring, view):
        arrive(ring, 0, view(left, 0))
        push(ring, 4, view(left, 0), right)
        arrive(ring, 1, view(right, 1))
        push(ring, 5, view(right, 1), left)

    def ring_share(ring, view):
        arrive(ring, 2, view(left, 1))
        push(ring, 7, view(left), sibling)
        arrive(ring, 3, view(right, 0))
        push(ring, 8, view(right), sibling)

    def ring_last(ring, view):
        arrive(ring, 4, view(across, 0))
        arrive(ring, 5, view(across, 1))
        push(ring, 9, view(across), sibling)

    def ring_end(ring, view):
        for n, u in ((6, t), (7, left), (8, right), (9, across)):
            arrive(ring, n, view(u // 2 * 2 + 1 - core))

    def give(s):
        def one(k, carry):
            f = partner(k)
            pick[s, f] = grads[code[slots * f + s] // 2].astype(pick.dtype)
            pltpu.make_async_remote_copy(
                src_ref=pick.at[s, f],
                dst_ref=g_full.at[s, g_rows, g_cols],
                send_sem=a2a_send.at[s],
                recv_sem=a2a_recv.at[s],
                device_id=to_owner(f),
            ).start()
            return carry

        lax.fori_loop(1, owners, one, 0)
        g_full[s, g_rows, g_cols] = grads[code[slots * me + s] // 2].astype(g_full.dtype)

    def taken(ref, count, sem):
        whole = ref.at[pl.ds(0, count)]
        pltpu.make_async_copy(whole, whole, sem).wait()

    def rows_here(s):
        taken(pick.at[s], owners - 1, a2a_recv.at[s])

    def squares(tile):
        return jnp.sum((tile * tile).reshape(-1, 8, col_share), axis=0)

    def preconditioned(s):
        half[s] = jnp.dot(
            g_full[s], root_right[s], preferred_element_type=jnp.float32
        ).astype(half.dtype)
        product = jnp.dot(rl_full[s], half[s], preferred_element_type=jnp.float32)
        dir_buf[s] = product.astype(dir_buf.dtype)
        dir_sum = squares(product)

        def one(k, carry):
            f = partner(k)
            pltpu.make_async_remote_copy(
                src_ref=dir_buf.at[s, pl.ds(pl.multiple_of(f * row_share, row_share), row_share)],
                dst_ref=back.at[slots * me + s],
                send_sem=back_send.at[s],
                recv_sem=back_recv.at[s],
                device_id=to_owner(f),
            ).start()
            return carry

        lax.fori_loop(1, owners, one, 0)
        back[slots * me + s] = dir_buf[s, g_rows]
        return dir_sum

    def tell(s, dir_sum):
        parts[s, t, 0:8] = dir_sum
        parts[s, t, 8:16] = squares(g_full[s, :, g_cols].astype(jnp.float32))

        def one(k, carry):
            pltpu.make_async_remote_copy(
                src_ref=parts.at[s, t],
                dst_ref=parts.at[s, t],
                send_sem=part_send.at[s],
                recv_sem=part_recv.at[s],
                device_id=to_peer((t + k) % peers),
            ).start()
            return carry

        lax.fori_loop(1, peers, one, 0)

    def scale_of(s):
        taken(parts.at[s], peers - 1, part_recv.at[s])
        total = jnp.sum(parts[s], axis=0)
        dir_sq = jnp.sum(total[0:8], keepdims=True)
        grad_sq = jnp.sum(total[8:16], keepdims=True)
        return jnp.sqrt(grad_sq / (dir_sq + graft_eps))

    def send_scales():
        lane = lax.broadcasted_iota(jnp.int32, (1, col_share), 1)
        scales[me] = jnp.where(lane < col_share // 2, scale_of(0), scale_of(1))

        def one(k, carry):
            f = partner(k)
            pltpu.make_async_remote_copy(
                src_ref=scales.at[me],
                dst_ref=scales.at[me],
                send_sem=scale_send,
                recv_sem=scale_recv,
                device_id=to_owner(f),
            ).start()
            return carry

        lax.fori_loop(1, owners, one, 0)

    def statistics(s):
        used = code[slots * me + s] % 2 == 1

        def left_tile(i, carry):
            cols = pl.ds(pl.multiple_of(i * TILE, TILE), TILE)
            prod = lax.dot_general(
                g_full[s, my_rows, :],
                g_full[s, cols, :],
                (((1,), (1,)), ((), ())),
                preferred_element_type=jnp.float32,
            )
            old = stat_left[s, :, cols].astype(jnp.float32)
            new = jnp.where(used, stat_decay * old + (1.0 - stat_decay) * prod, old)
            new_left[s, :, cols] = new.astype(new_left.dtype)
            return carry

        def right_tile(i, carry):
            cols = pl.ds(pl.multiple_of(i * TILE, TILE), TILE)
            prod = lax.dot_general(
                g_full[s, :, g_cols],
                g_full[s, :, cols],
                (((0,), (0,)), ((), ())),
                preferred_element_type=jnp.float32,
            )
            old = stat_right[s, :, cols].astype(jnp.float32)
            new = jnp.where(used, stat_decay * old + (1.0 - stat_decay) * prod, old)
            new_right[s, :, cols] = new.astype(new_right.dtype)
            return carry

        lax.fori_loop(0, order // TILE, left_tile, 0)
        lax.fori_loop(0, order // TILE, right_tile, 0)

    g0, g1, rl0, rl1 = (slots, g_part(0)), (slots + 1, g_part(1)), (0, rl_part(0)), (1, rl_part(1))

    loads[0].wait()
    ring_begin(*rl0)
    loads[1].wait()
    give(0)
    give(1)
    ring_forward(*rl0)
    ring_begin(*rl1)
    ring_share(*rl0)
    ring_last(*rl0)
    ring_forward(*rl1)
    ring_share(*rl1)
    rows_here(0)
    ring_begin(*g0)
    ring_last(*rl1)
    ring_forward(*g0)
    ring_share(*g0)
    ring_last(*g0)
    loads[2].wait()
    ring_end(*rl0)
    ring_end(*g0)
    rows_here(1)
    ring_begin(*g1)
    dir_sum = preconditioned(0)
    tell(0, dir_sum)
    ring_forward(*g1)
    ring_share(*g1)
    ring_last(*g1)
    ring_end(*rl1)
    ring_end(*g1)
    dir_sum = preconditioned(1)
    tell(1, dir_sum)
    loads[3].wait()
    loads[4].wait()
    statistics(0)
    send_scales()
    statistics(1)
    stores = [
        pltpu.make_async_copy(new_left, new_left_hbm, store_sem.at[0]),
        pltpu.make_async_copy(new_right, new_right_hbm, store_sem.at[1]),
    ]
    for store in stores:
        store.start()

    taken(scales, owners - 1, scale_recv)
    each = scales[:, 0, :]
    for s in range(slots):
        column = each[:, s * (col_share // 2) : s * (col_share // 2) + 1]
        scale_rows[s * owners : (s + 1) * owners, :] = jnp.broadcast_to(column, (owners, col_share))
    for s in range(slots):
        taken(back, owners - 1, back_recv.at[s])

    def choose(b, carry):
        slot = block_slot[b]
        scale = scale_rows[pl.ds(slot % slots * owners + slot // slots, 1), :]
        directions[b] = (back[slot].astype(jnp.float32) * scale).astype(directions.dtype)
        return carry

    lax.fori_loop(0, blocks, choose, 0)

    for store in stores:
        store.wait()
    taken(scales, owners - 1, scale_send)
    for s in range(slots):
        taken(pick.at[s], owners - 1, a2a_send.at[s])
        taken(back, owners - 1, back_send.at[s])
        taken(parts.at[s], peers - 1, part_send.at[s])
        for ring in (s, slots + s):
            sent = rl_full.at[s, pl.ds(0, 7 * rl_rows)]
            pltpu.make_async_copy(sent, sent, ring_send.at[ring]).wait()


def on_device(grads, block_slot, stat_left, stat_right, root_left, root_right):
    owners = lax.axis_size("fsdp")
    peers = lax.axis_size("tensor")
    blocks, row_share, col_share = grads.shape
    slots, left_rows, order = stat_left.shape
    slot_ids = jnp.arange(owners * slots, dtype=jnp.int32)
    block_ids = jnp.arange(blocks, dtype=jnp.int32)
    match = block_slot[None, :] == slot_ids[:, None]
    code = jnp.sum(jnp.where(match, 2 * block_ids[None, :] + 1, 0), axis=1, dtype=jnp.int32)
    smem = pl.BlockSpec(memory_space=pltpu.SMEM)
    vmem = pl.BlockSpec(memory_space=pltpu.VMEM)
    hbm = pl.BlockSpec(memory_space=pltpu.HBM)
    bf16 = jnp.bfloat16
    dma = pltpu.SemaphoreType.DMA
    return pl.pallas_call(
        functools.partial(kernel, owners, peers),
        out_shape=(
            jax.ShapeDtypeStruct(grads.shape, bf16),
            jax.ShapeDtypeStruct(stat_left.shape, bf16),
            jax.ShapeDtypeStruct(stat_right.shape, bf16),
        ),
        in_specs=[smem, smem] + [hbm] * 5,
        out_specs=(vmem, hbm, hbm),
        scratch_shapes=[
            pltpu.VMEM(grads.shape, grads.dtype),
            pltpu.VMEM(stat_left.shape, bf16),
            pltpu.VMEM(stat_right.shape, bf16),
            pltpu.VMEM(root_right.shape, bf16),
            pltpu.VMEM(stat_left.shape, bf16),
            pltpu.VMEM(stat_right.shape, bf16),
            pltpu.VMEM((slots, order, order), bf16),
            pltpu.VMEM((slots, order, order), bf16),
            pltpu.VMEM((slots, owners, row_share, col_share), bf16),
            pltpu.VMEM((slots, order, col_share), bf16),
            pltpu.VMEM((slots, order, col_share), bf16),
            pltpu.VMEM((slots * owners, row_share, col_share), bf16),
            pltpu.VMEM((slots, peers, 16, col_share), jnp.float32),
            pltpu.VMEM((owners, 1, col_share), jnp.float32),
            pltpu.VMEM((slots * owners, col_share), jnp.float32),
            dma((slots,)),
            dma((slots,)),
            dma((slots,)),
            dma((slots,)),
            dma((slots,)),
            dma((slots,)),
            dma(()),
            dma(()),
            dma((2 * slots,)),
            dma((2 * slots, 10)),
            dma((5,)),
            dma((2,)),
        ],
        compiler_params=pltpu.CompilerParams(
            collective_id=0, has_side_effects=True, vmem_limit_bytes=52 * 1024 * 1024
        ),
        name="shampoo_step",
    )(code, block_slot, grads, stat_left, stat_right, root_left, root_right)


def solution(mesh):
    placed = (
        P(None, "fsdp", "tensor"),
        P(),
        P("fsdp", "tensor", None),
        P("fsdp", "tensor", None),
        P("fsdp", "tensor", None),
        P("fsdp", None, "tensor"),
    )
    return jax.shard_map(
        on_device,
        mesh=mesh,
        in_specs=placed,
        out_specs=(P(None, "fsdp", "tensor"), P("fsdp", "tensor", None), P("fsdp", "tensor", None)),
        check_vma=False,
    )
```

time: 99.2 us -> 85.3 us (0.86)
  Pallas kernels: 89.9 us -> 80.4 us
  local copies, waits for them, and re-layouts: 8.13 us -> 3.97 us
    pallas_call x1, Pallas kernels: 89.9 us -> 80.4 us  [on_device(): pl.pallas_call(functools.partial(kernel, owners, peers), out_shape=(jax.S...]
    unnamed x15 -> x7, local copies, waits for them, and re-layouts: 8.13 us -> 3.97 us
where the time goes in v3:
time: 85.3 us; the launch traced here: 85.1 us
  Pallas kernels  80.4 us (94%)
  local copies, waits for them, and re-layouts  3.97 us (5%)
    pallas_call x1, Pallas kernels, on_device(): pl.pallas_call(functools.partial(kernel, owners, peers), out_shape=(jax.S...  80.4 us
    unnamed x7, local copies, waits for them, and re-layouts  3.97 us

profile of v3, /device:TPU:1, one launch (start us, length us, event | category | flops | bytes accessed | tf_op | source)
XLA Modules:
  0.0 85.1 jit_solution(2877962091473928888)
XLA Ops:
  0.6 0.0 copy-start.1
  0.7 0.6 copy-done.1
  1.3 0.1 select_reduce_fusion.code
  1.4 0.0 copy-start
  1.4 1.0 %copy-done = f32[64,16,128]{2,1,0:T(8,128)S(1)} copy-done((f32[64,16,128]{2,1,0:T(8,128)S(1)}, f32[64,16,128]{2,1,0:T(8,128)}, u32[]{:S(2)}) %copy-start) | copy-done | bytes 524312
  2.4 80.4 %shampoo_step.1 = (bf16[64,16,128]{2,1,0:T(8,128)(2,1)S(1)}, bf16[2,128,1024]{2,1,0:T(8,128)(2,1)S(1)}, bf16[2,128,1024]{2,1,0:T(8,128)(2,1)S(1)}) custom-call(s32[128]{0:T(128)S(1)} %select_reduce_fusion.code, s32[64]{0:T(128)S(1)} %copy-done.1, f32[64,16,128]{2,1,0:T(8,128)S(1)} %copy-done, bf16[2,128,1024]{2,1,0:T(8,128)(2,1)} %stat_left_hbm.1, ...), custom_call_target="tpu_custom_call" | custom-call | tf_op jit(solution)/shard_map/shampoo_step/pallas_call | solution.py:383
  82.8 0.7 copy.12
  83.6 0.8 copy.13
  84.3 0.8 copy.14
  (1 shorter events, 0.0 us)
Async XLA Ops:
  0.6 0.7 copy-start.1
  1.4 1.0 %copy-start = (f32[64,16,128]{2,1,0:T(8,128)S(1)}, f32[64,16,128]{2,1,0:T(8,128)}, u32[]{:S(2)}) copy-start(f32[64,16,128]{2,1,0:T(8,128)} %grads_hbm.1) | copy-start | bytes 1572868

commit v4 on v3

--- a/solution.py
+++ b/solution.py
@@ -36,6 +36,7 @@
     rl_full,
     pick,
     half,
+    half_sum,
     dir_buf,
     back,
     parts,
@@ -198,10 +199,25 @@
     def squares(tile):
         return jnp.sum((tile * tile).reshape(-1, 8, col_share), axis=0)
 
-    def preconditioned(s):
+    def half_whole(s):
         half[s] = jnp.dot(
             g_full[s], root_right[s], preferred_element_type=jnp.float32
         ).astype(half.dtype)
+
+    def half_part(s, u):
+        cols = pl.ds(pl.multiple_of(u // 2 * 2 * col_share, 2 * col_share), 2 * col_share)
+        return jnp.dot(
+            g_full[s, :, cols], root_right[s, cols, :], preferred_element_type=jnp.float32
+        )
+
+    def half_late(s, ring, view):
+        for n, u in ((6, t), (7, left), (8, right)):
+            arrive(ring, n, view(u // 2 * 2 + 1 - core))
+        half_sum[...] = half_part(s, t) + half_part(s, left) + half_part(s, right)
+        arrive(ring, 9, view(across // 2 * 2 + 1 - core))
+        half[s] = (half_sum[...] + half_part(s, across)).astype(half.dtype)
+
+    def preconditioned(s):
         product = jnp.dot(rl_full[s], half[s], preferred_element_type=jnp.float32)
         dir_buf[s] = product.astype(dir_buf.dtype)
         dir_sum = squares(product)
@@ -305,25 +321,26 @@
     ring_share(*rl0)
     ring_last(*rl0)
     ring_forward(*rl1)
-    ring_share(*rl1)
     rows_here(0)
     ring_begin(*g0)
+    ring_share(*rl1)
     ring_last(*rl1)
     ring_forward(*g0)
     ring_share(*g0)
+    rows_here(1)
+    ring_begin(*g1)
     ring_last(*g0)
     loads[2].wait()
     ring_end(*rl0)
     ring_end(*g0)
-    rows_here(1)
-    ring_begin(*g1)
+    half_whole(0)
     dir_sum = preconditioned(0)
     tell(0, dir_sum)
     ring_forward(*g1)
     ring_share(*g1)
     ring_last(*g1)
     ring_end(*rl1)
-    ring_end(*g1)
+    half_late(1, *g1)
     dir_sum = preconditioned(1)
     tell(1, dir_sum)
     loads[3].wait()
@@ -352,7 +369,7 @@
         directions[b] = (back[slot].astype(jnp.float32) * scale).astype(directions.dtype)
         return carry
 
-    lax.fori_loop(0, blocks, choose, 0)
+    lax.fori_loop(0, blocks, choose, 0, unroll=8)
 
     for store in stores:
         store.wait()
@@ -400,6 +417,7 @@
             pltpu.VMEM((slots, order, order), bf16),
             pltpu.VMEM((slots, owners, row_share, col_share), bf16),
             pltpu.VMEM((slots, order, col_share), bf16),
+            pltpu.VMEM((order, col_share), jnp.float32),
             pltpu.VMEM((slots, order, col_share), bf16),
             pltpu.VMEM((slots * owners, row_share, col_share), bf16),
             pltpu.VMEM((slots, peers, 16, col_share), jnp.float32),
@@ -419,7 +437,7 @@
             dma((2,)),
         ],
         compiler_params=pltpu.CompilerParams(
-            collective_id=0, has_side_effects=True, vmem_limit_bytes=52 * 1024 * 1024
+            collective_id=0, has_side_effects=True, vmem_limit_bytes=105 * 512 * 1024
         ),
         name="shampoo_step",
     )(code, block_slot, grads, stat_left, stat_right, root_left, root_right)

time: 85.3 us -> 83.1 us (0.974)
  Pallas kernels: 80.4 us -> 79.3 us
  local copies, waits for them, and re-layouts: 3.97 us -> 2.93 us
    pallas_call x1, Pallas kernels: 80.4 us -> 79.3 us  [on_device(): pl.pallas_call(functools.partial(kernel, owners, peers), out_shape=(jax.S...]
    unnamed x7 -> x5, local copies, waits for them, and re-layouts: 3.97 us -> 2.93 us
where the time goes in v4:
time: 83.1 us; the launch traced here: 83 us
  Pallas kernels  79.3 us (95%)
  local copies, waits for them, and re-layouts  2.93 us (4%)
    pallas_call x1, Pallas kernels, on_device(): pl.pallas_call(functools.partial(kernel, owners, peers), out_shape=(jax.S...  79.3 us
    unnamed x5, local copies, waits for them, and re-layouts  2.93 us

profile of v4, /device:TPU:1, one launch (start us, length us, event | category | flops | bytes accessed | tf_op | source)
XLA Modules:
  0.0 83.0 jit_solution(14838278051557604090)
XLA Ops:
  0.6 0.0 copy-start
  0.7 0.6 copy-done
  1.3 0.1 select_reduce_fusion.code
  1.4 79.3 %shampoo_step.1 = (bf16[64,16,128]{2,1,0:T(8,128)(2,1)S(1)}, bf16[2,128,1024]{2,1,0:T(8,128)(2,1)S(1)}, bf16[2,128,1024]{2,1,0:T(8,128)(2,1)S(1)}) custom-call(s32[128]{0:T(128)S(1)} %select_reduce_fusion.code, s32[64]{0:T(128)S(1)} %copy-done, f32[64,16,128]{2,1,0:T(8,128)} %grads_hbm.1, bf16[2,128,1024]{2,1,0:T(8,128)(2,1)} %stat_left_hbm.1, ...), custom_call_target="tpu_custom_call" | custom-call | tf_op jit(solution)/shard_map/shampoo_step/pallas_call | solution.py:400
  80.7 0.7 copy.12
  81.4 0.8 copy.13
  82.2 0.8 copy.14
  (1 shorter events, 0.0 us)
Async XLA Ops:
  0.6 0.7 copy-start

commit v5 on v4

--- a/solution.py
+++ b/solution.py
@@ -111,7 +111,7 @@
         pl.semaphore_signal(barrier, inc=1, device_id=to_peer((t + k) % peers))
         return carry
 
-    lax.fori_loop(1, owners, greet_owner, 0)
+    lax.fori_loop(1, owners, greet_owner, 0, unroll=9)
     lax.fori_loop(1, peers, greet_peer, 0)
     pl.semaphore_wait(barrier, owners + peers - 2)
 
@@ -166,12 +166,18 @@
 
     def ring_last(ring, view):
         arrive(ring, 4, view(across, 0))
+        push(ring, 9, view(across, 0), sibling)
         arrive(ring, 5, view(across, 1))
-        push(ring, 9, view(across), sibling)
+        push(ring, 10, view(across, 1), sibling)
+
+    def across_end(ring, view):
+        for part in range(2):
+            arrive(ring, 9 + part, view(across // 2 * 2 + 1 - core, part))
 
     def ring_end(ring, view):
-        for n, u in ((6, t), (7, left), (8, right), (9, across)):
+        for n, u in ((6, t), (7, left), (8, right)):
             arrive(ring, n, view(u // 2 * 2 + 1 - core))
+        across_end(ring, view)
 
     def give(s):
         def one(k, carry):
@@ -214,7 +220,7 @@
         for n, u in ((6, t), (7, left), (8, right)):
             arrive(ring, n, view(u // 2 * 2 + 1 - core))
         half_sum[...] = half_part(s, t) + half_part(s, left) + half_part(s, right)
-        arrive(ring, 9, view(across // 2 * 2 + 1 - core))
+        across_end(ring, view)
         half[s] = (half_sum[...] + half_part(s, across)).astype(half.dtype)
 
     def preconditioned(s):
@@ -432,7 +438,7 @@
             dma(()),
             dma(()),
             dma((2 * slots,)),
-            dma((2 * slots, 10)),
+            dma((2 * slots, 11)),
             dma((5,)),
             dma((2,)),
         ],

time: 83.1 us -> 83.4 us (level)
  no operation moved by 1% of the time
where the time goes in v5:
time: 83.4 us; the launch traced here: 83.3 us
  Pallas kernels  79.6 us (95%)
  local copies, waits for them, and re-layouts  2.93 us (4%)
    pallas_call x1, Pallas kernels, on_device(): pl.pallas_call(functools.partial(kernel, owners, peers), out_shape=(jax.S...  79.6 us
    unnamed x5, local copies, waits for them, and re-layouts  2.93 us

profile of v5, /device:TPU:1, one launch (start us, length us, event | category | flops | bytes accessed | tf_op | source)
XLA Modules:
  0.0 83.3 jit_solution(18359070354240010972)
XLA Ops:
  0.6 0.0 copy-start
  0.7 0.6 copy-done
  1.3 0.1 select_reduce_fusion.code
  1.4 79.6 %shampoo_step.1 = (bf16[64,16,128]{2,1,0:T(8,128)(2,1)S(1)}, bf16[2,128,1024]{2,1,0:T(8,128)(2,1)S(1)}, bf16[2,128,1024]{2,1,0:T(8,128)(2,1)S(1)}) custom-call(s32[128]{0:T(128)S(1)} %select_reduce_fusion.code, s32[64]{0:T(128)S(1)} %copy-done, f32[64,16,128]{2,1,0:T(8,128)} %grads_hbm.1, bf16[2,128,1024]{2,1,0:T(8,128)(2,1)} %stat_left_hbm.1, ...), custom_call_target="tpu_custom_call" | custom-call | tf_op jit(solution)/shard_map/shampoo_step/pallas_call | solution.py:406
  81.0 0.7 copy.12
  81.7 0.8 copy.13
  82.5 0.8 copy.14
  (1 shorter events, 0.0 us)
Async XLA Ops:
  0.6 0.7 copy-start
